TPU v7x, 32 devices: a whole 2x2x4 slice. The times are simulated.
32 devices in a mesh: grp: 2 (over y), epoch: 4 (over x, core), asset: 4 (over z).
Axes of the slice: x: 2, y: 2, z: 4, core: 2. Of those that a mesh axis runs over, the one named last changes fastest.
Arguments:
- signals: bfloat16 [8, 1024, 256], P(('grp', 'epoch'), 'asset'), parts along dimension 0, may hold values from -6 to 6
- targets: bfloat16 [8, 1024, 256], P(('grp', 'epoch'), 'asset'), parts along dimension 0, may hold values from -6 to 6
- row_counts: int32 [8, 4], P(('grp', 'epoch'), 'asset'), parts along dimension 0, may hold values from 32 to 256, as said below
- feature_weights: bfloat16 [256, 2048], replicated, may hold values from -0.375 to 0.375
- phases: float32 [2048], replicated, may hold values from -3.140625 to 3.140625
- spread_ids: int32 [2048], replicated, may hold values from 0 to 3
Outputs:
- coefficients: float32 [8, 2048, 256], P(('grp', 'epoch'), 'asset'), parts along dimension 0
There are 2 independent parts, one for each index of `grp`. A program takes and returns all parts, laid end to end along the dimension named above; an argument that names none is the same for every part. Nothing has to cross between parts.
Inputs may be any that keep to these rules, and one draw needn't show every extreme that they name: `row_counts`: each count is at least 32, and in every epoch some asset group has exactly 256 live rows.
All inputs are finite; a program needn't handle non-finite values.
Results may differ from a plain program's by a relative error of at most 0.0003.
Values may be sent and summed in bfloat16 or wider, within the bound.
A program may use at most 64 MiB of HBM per device.

v0:
```python
import jax
import jax.numpy as jnp
from jax import lax
from jax.sharding import PartitionSpec as P

ITERS = 3


ridge_penalty = 0.05
epsilon = 1e-06


def prefix(part, axis, combine, identity):
    place = lax.axis_index(axis)
    gathered = jax.tree.map(lambda a: lax.all_gather(a, axis), part)
    state = jax.tree.map(lambda a, e: jnp.zeros_like(a) + jnp.asarray(e, a.dtype), part, identity)

    def one(hop, state):
        return combine(
            state, jax.tree.map(lambda a: lax.dynamic_index_in_dim(a, hop, 0, False), gathered)
        )

    return lax.fori_loop(0, place, one, state)


def feature_scale(spread_ids):
    return (
        0.5
        * (
            1.0
            + jnp.where(spread_ids >= 1, 1.0, 0.0)
            + jnp.where(spread_ids >= 2, 2.0, 0.0)
            + jnp.where(spread_ids >= 3, 4.0, 0.0)
        )
    ).astype(jnp.float32)


def make_features(inputs, feature_weights, phases, spread_ids):
    projected = jnp.dot(inputs, feature_weights, preferred_element_type=jnp.float32)
    return jnp.sin(projected * feature_scale(spread_ids) + phases)


def add_pair(earlier, later):
    return (earlier[0] + later[0], earlier[1] + later[1])


def on_device(signals, targets, row_counts, feature_weights, phases, spread_ids):
    rows = signals.shape[1]
    width = feature_weights.shape[1]
    tgt_width = targets.shape[2]
    groups = lax.axis_size("asset")
    block_size = width // groups
    entries = width * tgt_width
    own_rows = row_counts[0, 0]
    all_counts = lax.all_gather(row_counts[0], "asset", axis=0, tiled=True)
    row_sum = jnp.sum(all_counts).astype(jnp.float32)
    inputs = signals[0]
    returns = targets[0]
    features = make_features(inputs, feature_weights, phases, spread_ids)
    live_mask = (jnp.arange(rows) < own_rows)[:, None]
    features = jnp.where(live_mask, features, jnp.zeros_like(features))
    returns = jnp.where(live_mask, returns.astype(jnp.float32), jnp.zeros((), jnp.float32))
    combined = jnp.concatenate([features, returns], axis=1)
    contract_rows = (((0,), (0,)), ((), ()))
    gram_block = lax.psum_scatter(
        lax.dot_general(features, combined, contract_rows, precision=lax.Precision.HIGHEST),
        "asset",
        scatter_dimension=0,
        tiled=True,
    )
    earlier, earlier_rows = prefix(
        (gram_block, row_sum),
        "epoch",
        add_pair,
        (jnp.zeros_like(gram_block), jnp.zeros((), jnp.float32)),
    )
    cumulative = earlier + gram_block
    row_total = earlier_rows + row_sum
    first_row = lax.axis_index("asset") * block_size
    diagonal = jnp.arange(width)[None, :] == first_row + jnp.arange(block_size)[:, None]
    system = cumulative[:, :width] / row_total + ridge_penalty * jnp.where(
        diagonal, 1.0, 0.0
    ).astype(jnp.float32)
    residual = cumulative[:, width:] / row_total
    coef = jnp.zeros((block_size, tgt_width), jnp.float32)
    for iteration in range(ITERS):
        image = jnp.zeros((block_size, tgt_width), jnp.float32) + jnp.dot(
            system,
            lax.all_gather(residual, "asset", axis=0, tiled=True),
            precision=lax.Precision.HIGHEST,
        )
        res_norm, res_curve = lax.psum(
            (jnp.sum(residual * residual), jnp.sum(residual * image)), "asset"
        )
        step_size = res_norm / entries / (res_curve / entries + epsilon)
        coef = coef + step_size * residual
        residual = residual - step_size * image
    return (jnp.sqrt(row_total) * coef)[None]


def solution(mesh):
    placed = (
        P(("grp", "epoch"), "asset", None),
        P(("grp", "epoch"), "asset", None),
        P(("grp", "epoch"), "asset"),
        P(),
        P(),
        P(),
    )
    return jax.shard_map(
        on_device,
        mesh=mesh,
        in_specs=placed,
        out_specs=P(("grp", "epoch"), "asset", None),
        check_vma=False,
    )
```

profile of v0, /device:TPU:11, one launch (start us, length us, event | category | flops | bytes accessed | tf_op | source)
XLA Modules:
  0.0 706.9 jit_solution(8003672284095175270)
XLA Ops:
  7.3 0.7 add_multiply_fusion
  8.0 1.0 convert_select_fusion
  9.0 8.1 %fusion.3 = f32[256,2048]{1,0:T(8,128)S(1)} fusion(bf16[256,2048]{1,0:T(8,128)(2,1)S(1)} %copy-done, f32[2048]{0:T(1024)} %param.12, f32[2048]{0:T(1024)S(1)} %add_multiply_fusion, pred[256]{0:T(512)(128)(4,1)S(1)} %iota_compare_fusion.1, bf16[1,256,256]{2,1,0:T(8,128)(2,1)} %param.8), kind=kOutput, calls=%fused_computation.7 | convolution fusion | flops 270008320 | bytes 3293440 | tf_op jit(solution)/shard_map/dot_general | solution.py:39
  17.1 19.4 %fusion.4 = f32[2048,2304]{1,0:T(8,128)} fusion(f32[256,2048]{1,0:T(8,128)S(1)} %fusion.3, f32[256,256]{1,0:T(8,128)S(1)} %convert_select_fusion), kind=kOutput, calls=%fused_computation.8 | convolution fusion | flops 14496104448 | bytes 21233664 | tf_op jit(solution)/shard_map/dot_general | solution.py:66
  36.6 312.0 %reduce-scatter.2.cloned.1.call-done = f32[512,2304]{1,0:T(8,128)} async-done(((f32[2048,2304]{1,0:T(8,128)}), f32[512,2304]{1,0:T(8,128)}) %reduce-scatter.2.cloned.1.call-update) | async-done | bytes 4718608 | tf_op jit(solution)/shard_map/reduce_scatter | solution.py:65
  349.9 9.4 %all-reduce = s32[4]{0:T(128)S(1)} all-reduce(s32[4]{0:T(128)S(1)} %bitcast_dynamic-update-slice_fusion), channel_id=3, replica_groups=mesh['grp'=2,'epoch'=4,'asset'=4] {'asset'}, use_global_device_ids=true, to_apply=%add | all-reduce | flops 4 | bytes 32
  361.2 0.8 dynamic-update-slice.1
  361.9 7.6 %all-reduce.1 = f32[4]{0:T(128)S(1)} all-reduce(f32[4]{0:T(128)S(1)} %dynamic-update-slice.1), channel_id=1, replica_groups=mesh['grp'=2,'epoch'=4,'asset'=4] {'epoch'}, use_global_device_ids=true, to_apply=%add.1 | all-reduce | flops 4 | bytes 32
  369.6 104.3 %all-gather.13.cloned.1.call-done = f32[2048,2304]{1,0:T(8,128)} async-done(((f32[512,2304]{1,0:T(8,128)}), f32[2048,2304]{1,0:T(8,128)}) %all-gather.13.cloned.1.call-update) | async-done | bytes 18874384 | tf_op jit(solution)/shard_map/all_gather | solution.py:15
  473.9 2.5 broadcast_in_dim.58
  476.4 23.6 %while.12 = (s32[]{:T(128)}, f32[512,2304]{1,0:T(8,128)}, f32[]{:T(128)}, s32[]{:T(128)}, f32[4,512,2304]{2,1,0:T(8,128)}, /*index=5*/f32[4]{0:T(128)S(1)}, s32[]{:T(128)}, s32[]{:T(128)}, s32[]{:T(128)}) while((s32[]{:T(128)}, f32[512,2304]{1,0:T(8,128)}, f32[]{:T(128)}, s32[]{:T(128)}, f32[4,512,2304]{2,1,0:T(8,128)}, ...), condition=%wide.region_3.4_spmd, body=%wide.region_2.3_spmd.sunk | while | flops 1179654 | bytes 14155931 | solution.py:23
  476.4 6.6 bitcast_add_fusion.2
  483.0 0.6 dynamic_slice.12
  484.3 6.6 bitcast_add_fusion.2
  490.9 0.6 dynamic_slice.12
  492.2 6.6 bitcast_add_fusion.2
  500.1 4.3 add.88
  504.4 2.1 copy-done.2
  506.5 0.8 slice_divide_fusion.1
  507.4 5.1 fusion
  512.6 39.4 %all-gather.7.cloned.1.call-done = f32[2048,256]{1,0:T(8,128)} async-done(((f32[512,256]{1,0:T(8,128)}), f32[2048,256]{1,0:T(8,128)}) %all-gather.7.cloned.1.call-update) | async-done | bytes 2097168 | tf_op jit(solution)/shard_map/all_gather | solution.py:89
  552.0 6.6 multiply_reduce_fusion.3
  558.6 9.3 %all-reduce.4 = (f32[]{:T(128)}, f32[]{:T(128)}) all-reduce(f32[]{:T(128)} %get-tuple-element.44, f32[]{:T(128)} %get-tuple-element.43), channel_id=1, replica_groups=mesh['grp'=2,'epoch'=4,'asset'=4] {'asset'}, use_global_device_ids=true, to_apply=%region_5.6 | all-reduce | flops 2 | bytes 16 | tf_op jit(solution)/shard_map/psum | solution.py:92
  569.3 1.9 multiply_subtract_fusion.1
  571.5 45.1 %all-gather.9.cloned.1.call-done = f32[2048,256]{1,0:T(8,128)} async-done(((f32[512,256]{1,0:T(8,128)}), f32[2048,256]{1,0:T(8,128)}) %all-gather.9.cloned.1.call-update) | async-done | bytes 2097168 | tf_op jit(solution)/shard_map/all_gather | solution.py:89
  616.5 6.9 multiply_reduce_fusion.1
  623.5 9.3 %all-reduce.3 = (f32[]{:T(128)}, f32[]{:T(128)}) all-reduce(f32[]{:T(128)} %get-tuple-element.42, f32[]{:T(128)} %get-tuple-element.41), channel_id=1, replica_groups=mesh['grp'=2,'epoch'=4,'asset'=4] {'asset'}, use_global_device_ids=true, to_apply=%region_9.10 | all-reduce | flops 2 | bytes 16 | tf_op jit(solution)/shard_map/psum | solution.py:92
  634.2 1.4 multiply_reduce_fusion
  635.7 45.3 %all-gather.11.cloned.1.call-done = f32[2048,256]{1,0:T(8,128)} async-done(((f32[512,256]{1,0:T(8,128)}), f32[2048,256]{1,0:T(8,128)}) %all-gather.11.cloned.1.call-update) | async-done | bytes 2097168 | tf_op jit(solution)/shard_map/all_gather | solution.py:89
  681.0 6.9 fusion.8
  687.9 9.3 %all-reduce.2 = (f32[]{:T(128)}, f32[]{:T(128)}) all-reduce(f32[]{:T(128)} %get-tuple-element.63, f32[]{:T(128)} %fusion.8), channel_id=1, replica_groups=mesh['grp'=2,'epoch'=4,'asset'=4] {'asset'}, use_global_device_ids=true, to_apply=%region_13.14 | all-reduce | flops 2 | bytes 16 | tf_op jit(solution)/shard_map/psum | solution.py:92
  698.4 2.0 multiply_bitcast_fusion
  (34 shorter events, 3.6 us)
Async XLA Ops:
  6.5 2.5 copy-start
  6.5 342.1 %reduce-scatter.2.cloned.1.call-start = ((), (), s32[]{:S(2)}) async-start(), calls=%async_computation.1 | async-start | bytes 23592960 | tf_op jit(solution)/shard_map/reduce_scatter | solution.py:65
  36.5 312.2 %copy-start.7 = (u32[32]{0:T(128)S(1)}, u32[32]{0:T(128)}, u32[]{:S(2)}) copy-start(u32[32]{0:T(128)} %constant.59) | copy-start | bytes 388
  36.6 324.0 %copy-start.6 = (u32[32]{0:T(128)S(1)}, u32[32]{0:T(128)}, u32[]{:S(2)}) copy-start(u32[32]{0:T(128)} %constant.64) | copy-start | bytes 388
  36.6 437.3 %all-gather.13.cloned.1.call-start = ((), (), s32[]{:S(2)}) async-start(), calls=%async_computation.5 | async-start | bytes 23592960 | tf_op jit(solution)/shard_map/all_gather | solution.py:15
  348.6 203.3 %all-gather.7.cloned.1.call-start = ((), (), s32[]{:S(2)}) async-start(), calls=%async_computation.2 | async-start | bytes 2621440 | tf_op jit(solution)/shard_map/all_gather | solution.py:89
  504.4 2.1 copy-start.2
  507.4 109.2 %all-gather.9.cloned.1.call-start = ((), (), s32[]{:S(2)}) async-start(), calls=%async_computation.3 | async-start | bytes 2621440 | tf_op jit(solution)/shard_map/all_gather | solution.py:89
  507.4 44.6 %copy-start.5 = (f32[512,256]{1,0:T(8,128)S(1)}, f32[512,256]{1,0:T(8,128)}, u32[]{:S(2)}) copy-start(f32[512,256]{1,0:T(8,128)} %slice_divide_fusion.1) | copy-start | bytes 1572868
  571.2 63.0 %copy-start.3 = (f32[512,256]{1,0:T(8,128)S(1)}, f32[512,256]{1,0:T(8,128)}, u32[]{:S(2)}) copy-start(f32[512,256]{1,0:T(8,128)} %multiply_subtract_fusion.1) | copy-start | bytes 1572868
  571.2 109.8 %all-gather.11.cloned.1.call-start = ((), (), s32[]{:S(2)}) async-start(), calls=%async_computation.4 | async-start | bytes 2621440 | tf_op jit(solution)/shard_map/all_gather | solution.py:89
  635.6 62.8 %copy-start.4 = (f32[512,256]{1,0:T(8,128)S(1)}, f32[512,256]{1,0:T(8,128)}, u32[]{:S(2)}) copy-start(f32[512,256]{1,0:T(8,128)} %get-tuple-element.64) | copy-start | bytes 1572868
  635.6 64.8 %copy-start.1 = (bf16[256,2048]{1,0:T(8,128)(2,1)S(1)}, bf16[256,2048]{1,0:T(8,128)(2,1)}, u32[]{:S(2)}) copy-start(bf16[256,2048]{1,0:T(8,128)(2,1)} %param.11) | copy-start | bytes 3145732
Sparse Core Ops, SparseCore 0:
  36.7 311.9 reduce-scatter.1
  350.3 123.5 all-gather.12
  507.5 44.4 all-gather.6
  571.3 45.1 all-gather.8
  635.7 45.1 all-gather.10
where the time goes:
time: 712 us; the launch traced here: 707 us
  waiting for transfers between devices  546 us (77%)
  matrix products  48 us (7%)
  blocking collectives  45 us (6%)
  other arithmetic  37.6 us (5%)
  between operations  18.6 us (3%)
  local copies, waits for them, and re-layouts  9.17 us (1%)
    reduce_scatter x1, waiting for transfers between devices, on_device(): lax.psum_scatter(lax.dot_general(features, combined, contract_rows, preci...  312 us
    all_gather x3, waiting for transfers between devices, on_device(): lax.all_gather(residual, 'asset', axis=0, tiled=True)  130 us
    all_gather x1, waiting for transfers between devices, prefix(): gathered = jax.tree.map(lambda a: lax.all_gather(a, axis), part)  104 us
    psum x3, blocking collectives, on_device(): lax.psum((jnp.sum(residual * residual), jnp.sum(residual * image)), 'asset')  28 us
    dot_general x3, matrix products, on_device(): jnp.dot(system, lax.all_gather(residual, 'asset', axis=0, tiled=True), pr...  20.5 us
    add x3, other arithmetic, add_pair(): return (earlier[0] + later[0], earlier[1] + later[1])  19.7 us
    dot_general x1, matrix products, on_device(): lax.dot_general(features, combined, contract_rows, precision=lax.Precisio...  19.4 us
    unnamed x2, blocking collectives  17 us
  transfers between devices with their start and end apart: 5, of which 5 were waited for; matrix products, arithmetic and copies ran while one was open for 1% of the time, Pallas kernels for 0%

commit v1 on v0

--- a/solution.py
+++ b/solution.py
@@ -1,6 +1,11 @@
+import functools
+import math
+
 import jax
 import jax.numpy as jnp
 from jax import lax
+from jax.experimental import pallas as pl
+from jax.experimental.pallas import tpu as pltpu
 from jax.sharding import PartitionSpec as P
 
 ITERS = 3
@@ -98,7 +103,357 @@
     return (jnp.sqrt(row_total) * coef)[None]
 
 
+MESH = pl.DeviceIdType.MESH
+MASK_ROWS = 16
+COS = (
+    1.0,
+    -19.73920440673828,
+    64.93911743164062,
+    -85.45011138916016,
+    60.16743087768555,
+    -25.96688461303711,
+    6.527706146240234,
+)
+NT = (((1,), (1,)), ((), ()))
+
+
+def mm(a, b):
+    return jnp.dot(a, b, preferred_element_type=jnp.float32)
+
+
+def mm_nt(a, b):
+    return lax.dot_general(a, b, NT, preferred_element_type=jnp.float32)
+
+
+def split(a):
+    high = a.astype(jnp.bfloat16)
+    return high, (a - high.astype(jnp.float32)).astype(jnp.bfloat16)
+
+
+def kernel(
+    X, Z, chunk, entries,
+    sig_ref, yt_ref, w_ref, sc_ref, ph_ref, out_ref,
+    sig_all, yt_all, hi, lo, proj, lhs, msk, vec, coef, vs, ust, own, got, totals, got_totals,
+    scal, last, outbox, landing,
+    gs_send, gs_recv, gy_send, gy_recv, ex_send, ex_recv, t_send, t_recv,
+    sc_send, sc_recv, la_send, la_recv, o_send, o_recv,
+):
+    rows, K = sig_ref.shape
+    F = w_ref.shape[1]
+    cols = yt_ref.shape[1] - MASK_ROWS
+    C = 2 * cols
+    B = X * Z
+    n = B * rows
+    nch = F // chunk
+    f32 = jnp.float32
+    epoch = lax.axis_index("epoch")
+    z = lax.axis_index("asset")
+    x = epoch // 2
+    core = epoch % 2
+    mate = 2 * x + (1 - core)
+
+    def at(xx, cc, zz):
+        return {"epoch": 2 * xx + cc, "asset": zz}
+
+    barrier = pltpu.get_barrier_semaphore()
+    peers = []
+    for d in range(1, B):
+        peers.append(at(lax.rem(x + d // Z, X), core, lax.rem(z + d % Z, Z)))
+    for d in range(Z):
+        peers.append(at(x, 1 - core, lax.rem(z + d, Z)))
+    for peer in peers:
+        pl.semaphore_signal(barrier, inc=1, device_id=peer, device_id_type=MESH)
+    pl.semaphore_wait(barrier, len(peers))
+
+    mine = x * Z + z
+
+    def sig_copy(d):
+        xx, zz = lax.rem(x + d // Z, X), lax.rem(z + d % Z, Z)
+        return pltpu.make_async_remote_copy(
+            src_ref=sig_ref, dst_ref=sig_all.at[mine],
+            send_sem=gs_send.at[d], recv_sem=gs_recv.at[d],
+            device_id=at(xx, core, zz), device_id_type=MESH)
+
+    def y_copy(d):
+        xx, zz = lax.rem(x + d // Z, X), lax.rem(z + d % Z, Z)
+        return pltpu.make_async_remote_copy(
+            src_ref=yt_ref.at[zz], dst_ref=yt_all.at[mine],
+            send_sem=gy_send.at[d], recv_sem=gy_recv.at[d],
+            device_id=at(xx, core, zz), device_id_type=MESH)
+
+    for d in range(1, B):
+        sig_copy(d).start()
+        y_copy(d).start()
+    sig_all[mine] = sig_ref[...]
+    yt_all[mine] = yt_ref[z]
+
+    def block(d, carry):
+        @pl.when(d > 0)
+        def _():
+            sig_copy(d).wait()
+            y_copy(d).wait()
+
+        xx = lax.rem(x + X - d // Z, X)
+        zz = lax.rem(z + Z - lax.rem(d, Z), Z)
+        slot = xx * Z + zz
+        base = pl.multiple_of(slot * rows, rows)
+        live = yt_all[slot, cols:cols + MASK_ROWS, :].astype(f32)[0:1, :]
+        y = yt_all[slot, 0:cols, :].astype(f32)
+        for q in range(2):
+            allow = jnp.where(2 * xx + core <= 2 * x + q, 1.0, 0.0).astype(f32)
+            msk[q, :, pl.ds(base, rows)] = jnp.broadcast_to(live * allow, (8, rows))
+            lhs[q * cols:(q + 1) * cols, pl.ds(base, rows)] = (y * allow).astype(jnp.bfloat16)
+        for k in range(nch):
+            part = slice(k * chunk, (k + 1) * chunk)
+            proj[:, part] = mm(sig_all[slot], w_ref[:, part])
+        for k in range(nch):
+            part = slice(k * chunk, (k + 1) * chunk)
+            scale = sc_ref[:, part]
+            phase = ph_ref[:, part]
+
+            def strip(r, carry):
+                r0 = pl.multiple_of(r * 16, 16)
+                t = proj[pl.ds(r0, 16), part] * scale + phase
+                f = t - jnp.round(t)
+                s = f * f
+                acc = s * COS[-1] + COS[-2]
+                for c in COS[-3::-1]:
+                    acc = acc * s + c
+                high, low = split(acc)
+                to = pl.ds(pl.multiple_of(base + r0, 16), 16)
+                hi[to, part] = high
+                lo[to, part] = low
+                return carry
+
+            lax.fori_loop(0, rows // 16, strip, 0, unroll=4)
+        return carry
+
+    lax.fori_loop(0, B, block, 0)
+
+    is_first = lax.broadcasted_iota(jnp.int32, (C, 1), 0) < cols
+
+    def spread(a0, a1):
+        return jnp.where(is_first, a0, a1)
+
+    totals[...] = jnp.zeros_like(totals)
+    for q in range(2):
+        totals[q] = jnp.broadcast_to(jnp.sum(msk[q], axis=1, keepdims=True), totals.shape[1:])
+    count_copy = pltpu.make_async_remote_copy(
+        src_ref=totals, dst_ref=got_totals, send_sem=t_send, recv_sem=t_recv,
+        device_id=at(x, 1 - core, z), device_id_type=MESH)
+    count_copy.start()
+
+    def exchange(s, k):
+        return pltpu.make_async_remote_copy(
+            src_ref=own.at[s, k], dst_ref=got.at[s, k],
+            send_sem=ex_send.at[s, k], recv_sem=ex_recv.at[s, k],
+            device_id=at(x, 1 - core, z), device_id_type=MESH)
+
+    for k in range(nch):
+        part = slice(k * chunk, (k + 1) * chunk)
+        own[0, k] = mm(lhs[...], hi[:, part]) + mm(lhs[...], lo[:, part])
+        exchange(0, k).start()
+    count_copy.wait()
+    count = [totals[q][0:1, 0:1] + got_totals[q][0:1, 0:1] for q in range(2)]
+    inverse = spread(1.0 / count[0], 1.0 / count[1])
+
+    norm = jnp.zeros((C, 1), f32)
+    for k in range(nch):
+        part = slice(k * chunk, (k + 1) * chunk)
+        exchange(0, k).wait()
+        v = (own[0, k] + got[0, k]) * inverse
+        vec[:, part] = v
+        high, low = split(v)
+        vs[0:C, part] = high
+        vs[C:2 * C, part] = low
+        norm = norm + jnp.sum(v * v, axis=1, keepdims=True)
+
+    tile_row = lax.broadcasted_iota(jnp.int32, (8, 128), 0)
+
+    def tile(norm, curve):
+        out = jnp.zeros((8, 128), f32)
+        for i, a in enumerate((norm[0:cols], norm[cols:], curve[0:cols], curve[cols:])):
+            out = jnp.where(tile_row == i, jnp.sum(a, axis=0, keepdims=True), out)
+        return out
+
+    def step_of(a):
+        res_norm = spread(a[0:1, 0:1], a[1:2, 0:1])
+        res_curve = spread(a[2:3, 0:1], a[3:4, 0:1])
+        return res_norm / entries / (res_curve / entries + epsilon)
+
+    for it in range(ITERS):
+        final = it == ITERS - 1
+
+        def forward(j, total):
+            base = pl.multiple_of(j * rows, rows)
+            here = pl.ds(base, rows)
+            u = mm_nt(vs[...], hi[here, :])
+            u = u[0:C] + u[C:] + mm_nt(vs[0:C, :], lo[here, :])
+            u = jnp.concatenate(
+                [u[0:cols] * msk[0, 0:1, here], u[cols:] * msk[1, 0:1, here]], axis=0)
+            if final:
+                return total + jnp.sum(u * u, axis=1, keepdims=True)
+            high, low = split(u)
+            ust[0:C, here] = high
+            ust[C:2 * C, here] = low
+            return total
+
+        square = lax.fori_loop(0, B, forward, jnp.zeros((C, 1), f32))
+        if final:
+            last[core * Z + z] = tile(norm, square)
+            copies = []
+            for d in range(1, 2 * Z):
+                cc, zz = lax.rem(core + d // Z, 2), lax.rem(z + d % Z, Z)
+                copies.append(pltpu.make_async_remote_copy(
+                    src_ref=last.at[core * Z + z], dst_ref=last.at[core * Z + z],
+                    send_sem=la_send.at[d], recv_sem=la_recv.at[d],
+                    device_id=at(x, cc, zz), device_id_type=MESH))
+            for copy in copies:
+                copy.start()
+            for copy in copies:
+                copy.wait()
+            a = last[0]
+            for i in range(1, 2 * Z):
+                a = a + last[i]
+            norms = spread(a[0:1, 0:1], a[1:2, 0:1]) * 0.5
+            curve = spread(a[2:3, 0:1] / count[0], a[3:4, 0:1] / count[1]) + ridge_penalty * norms
+            step = norms / entries / (curve / entries + epsilon)
+            root = spread(jnp.sqrt(count[0]), jnp.sqrt(count[1]))
+            for k in range(nch):
+                part = slice(k * chunk, (k + 1) * chunk)
+                coef[:, part] = (coef[:, part] + step * vec[:, part]) * root
+        else:
+            s = it + 1
+            for k in range(nch):
+                part = slice(k * chunk, (k + 1) * chunk)
+                image = mm(ust[...], hi[:, part])
+                own[s, k] = image[0:C] + image[C:] + mm(ust[0:C, :], lo[:, part])
+                exchange(s, k).start()
+            curve = jnp.zeros((C, 1), f32)
+            for k in range(nch):
+                part = slice(k * chunk, (k + 1) * chunk)
+                exchange(s, k).wait()
+                v = vec[:, part]
+                image = (own[s, k] + got[s, k]) * inverse + ridge_penalty * v
+                proj[0:C, part] = image
+                curve = curve + jnp.sum(v * image, axis=1, keepdims=True)
+            scal[it, z] = tile(norm, curve)
+            copies = []
+            for d in range(1, Z):
+                copies.append(pltpu.make_async_remote_copy(
+                    src_ref=scal.at[it, z], dst_ref=scal.at[it, z],
+                    send_sem=sc_send.at[it, d], recv_sem=sc_recv.at[it, d],
+                    device_id=at(x, core, lax.rem(z + d, Z)), device_id_type=MESH))
+            for copy in copies:
+                copy.start()
+            for copy in copies:
+                copy.wait()
+            a = scal[it, 0]
+            for i in range(1, Z):
+                a = a + scal[it, i]
+            step = step_of(a)
+            norm = jnp.zeros((C, 1), f32)
+            for k in range(nch):
+                part = slice(k * chunk, (k + 1) * chunk)
+                v = vec[:, part]
+                coef[:, part] = step * v if it == 0 else coef[:, part] + step * v
+                v = v - step * proj[0:C, part]
+                vec[:, part] = v
+                high, low = split(v)
+                vs[0:C, part] = high
+                vs[C:2 * C, part] = low
+                norm = norm + jnp.sum(v * v, axis=1, keepdims=True)
+
+    width = F // Z
+    first = pl.multiple_of(core * cols, cols)
+    for b in range(Z):
+        outbox[b] = coef[pl.ds(first, cols), b * width:(b + 1) * width]
+    copies = []
+    for d in range(1, Z):
+        zz = lax.rem(z + d, Z)
+        copies.append(pltpu.make_async_remote_copy(
+            src_ref=outbox.at[zz], dst_ref=landing.at[z],
+            send_sem=o_send.at[d], recv_sem=o_recv.at[d],
+            device_id=at(x, core, zz), device_id_type=MESH))
+    for copy in copies:
+        copy.start()
+    landing[z] = outbox[z]
+    for copy in copies:
+        copy.wait()
+    out_ref[...] = landing[...].reshape(Z * cols, width)
+
+
+def scratch_of(X, Z, rows, K, F, cols, chunk):
+    B = X * Z
+    n = B * rows
+    C = 2 * cols
+    nch = F // chunk
+    f32, bf16 = jnp.float32, jnp.bfloat16
+    buffers = [
+        ((B, rows, K), bf16), ((B, cols + MASK_ROWS, rows), bf16),
+        ((n, F), bf16), ((n, F), bf16), ((max(rows, C), F), f32), ((C, n), bf16),
+        ((2, 8, n), f32), ((C, F), f32), ((C, F), f32), ((2 * C, F), bf16), ((2 * C, n), bf16),
+        ((ITERS, nch, C, chunk), f32), ((ITERS, nch, C, chunk), f32),
+        ((2, 8, 128), f32), ((2, 8, 128), f32),
+        ((ITERS, Z, 8, 128), f32), ((2 * Z, 8, 128), f32),
+        ((Z, cols, F // Z), f32), ((Z, cols, F // Z), f32),
+    ]
+    held = sum(math.prod(shape) * jnp.dtype(dtype).itemsize for shape, dtype in buffers)
+    sems = [(B,)] * 4 + [(ITERS, nch)] * 2 + [()] * 2 + [(ITERS, Z)] * 2 + [(2 * Z,)] * 2 + [(Z,)] * 2
+    return buffers, sems, held
+
+
+VMEM_BUDGET = 44 * 2**20
+
+
+def plan(E, Z, rows, K, F, T):
+    if E % 2 or T % Z or F % Z:
+        return None
+    cols, chunk = T // Z, 512
+    if cols % 16 or rows % 128 or F % chunk or (F // Z) % 128 or K % 128:
+        return None
+    buffers, sems, held = scratch_of(E // 2, Z, rows, K, F, cols, chunk)
+    if held > VMEM_BUDGET:
+        return None
+    return cols, chunk, buffers, sems
+
+
+def fused(signals, targets, row_counts, feature_weights, phases, spread_ids):
+    E, Z = lax.axis_size("epoch"), lax.axis_size("asset")
+    rows, K = signals.shape[1:]
+    F = feature_weights.shape[1]
+    T = targets.shape[2]
+    cols, chunk, buffers, sems = plan(E, Z, rows, K, F, T)
+    live = jnp.arange(rows) < row_counts[0, 0]
+    returns = jnp.where(live[:, None], targets[0], jnp.zeros((), targets.dtype)).T
+    returns = returns.reshape(Z, cols, rows)
+    mask = jnp.broadcast_to(live.astype(targets.dtype), (Z, MASK_ROWS, rows))
+    returns = jnp.concatenate([returns, mask], axis=1)
+    turn = 1.0 / (2.0 * math.pi)
+    scale = (feature_scale(spread_ids) * turn)[None, :]
+    phase = (phases * turn - 0.25)[None, :]
+    vmem = pl.BlockSpec(memory_space=pltpu.VMEM)
+    out = pl.pallas_call(
+        functools.partial(kernel, E // 2, Z, chunk, float(F * T)),
+        out_shape=jax.ShapeDtypeStruct((T, F // Z), jnp.float32),
+        in_specs=[vmem] * 5,
+        out_specs=vmem,
+        scratch_shapes=[pltpu.VMEM(s, d) for s, d in buffers]
+        + [pltpu.SemaphoreType.DMA(s) if s else pltpu.SemaphoreType.DMA for s in sems],
+        compiler_params=pltpu.CompilerParams(
+            collective_id=0, has_side_effects=True, vmem_limit_bytes=56 * 2**20),
+    )(signals[0], returns, feature_weights, scale, phase)
+    return out.T[None]
+
+
 def solution(mesh):
+    def run(signals, targets, row_counts, feature_weights, phases, spread_ids):
+        fits = plan(
+            mesh.shape["epoch"], mesh.shape["asset"], signals.shape[1],
+            signals.shape[2], feature_weights.shape[1], targets.shape[2])
+        body = fused if fits else on_device
+        return body(signals, targets, row_counts, feature_weights, phases, spread_ids)
+
     placed = (
         P(("grp", "epoch"), "asset", None),
         P(("grp", "epoch"), "asset", None),
@@ -108,7 +463,7 @@
         P(),
     )
     return jax.shard_map(
-        on_device,
+        run,
         mesh=mesh,
         in_specs=placed,
         out_specs=P(("grp", "epoch"), "asset", None),

time: 712 us -> 108 us (0.15)
  waiting for transfers between devices: 546 us -> 0 us
  Pallas kernels: 0 us -> 99.8 us
  matrix products: 48 us -> 0 us
  blocking collectives: 45 us -> 0 us
  other arithmetic: 37.6 us -> 2.88 us
  between operations: 18.6 us -> 0.7 us
    reduce_scatter x1 -> x0, waiting for transfers between devices: 312 us -> none  [on_device(): lax.psum_scatter(lax.dot_general(features, combined, contract_rows, preci...]
    all_gather x4 -> x0, waiting for transfers between devices: 234 us -> none  [the longest x3 130 us: on_device(): lax.all_gather(residual, 'asset', axis=0, tiled=True)]
    pallas_call x0 -> x1, Pallas kernels: none -> 99.8 us  [fused(): pl.pallas_call(functools.partial(kernel, E // 2, Z, chunk, float(F * T)),...]
    dot_general x5 -> x0, matrix products: 48 us -> none  [the longest x3 20.5 us: on_device(): jnp.dot(system, lax.all_gather(residual, 'asset', axis=0, tiled=True), pr...]
    add x6 -> x0, other arithmetic: 29.1 us -> none  [the longest x3 19.7 us: add_pair(): return (earlier[0] + later[0], earlier[1] + later[1])]
    psum x3 -> x0, blocking collectives: 28 us -> none  [on_device(): lax.psum((jnp.sum(residual * residual), jnp.sum(residual * image)), 'asset')]
    unnamed x2 -> x0, blocking collectives: 17 us -> none
  transfers between devices with their start and end apart: 5 -> 0, of which waited for: 5 -> 0; matrix products, arithmetic and copies ran while one was open for 1% -> 0% of each run, Pallas kernels for 0% -> 0%
where the time goes in v1:
time: 108 us; the launch traced here: 106 us
  Pallas kernels  99.8 us (92%)
  other arithmetic  2.88 us (3%)
  local copies, waits for them, and re-layouts  2.26 us (2%)
    pallas_call x1, Pallas kernels, fused(): pl.pallas_call(functools.partial(kernel, E // 2, Z, chunk, float(F * T)),...  99.8 us

profile of v1, /device:TPU:11, one launch (start us, length us, event | category | flops | bytes accessed | tf_op | source)
XLA Modules:
  0.0 105.7 jit_solution(15546339168264911845)
XLA Ops:
  0.0 0.0 copy-start
  0.7 0.0 copy-done
  0.7 0.0 copy-start.1
  0.7 0.6 multiply_add_fusion
  1.3 0.1 copy-done.1
  1.4 0.6 add_multiply_fusion
  2.0 1.0 fusion
  3.0 0.1 copy.7
  3.1 0.7 pad_maximum_fusion.yt_ref
  3.8 99.8 %shard_map.64 = f32[256,512]{1,0:T(8,128)} custom-call(bf16[256,256]{1,0:T(8,128)(2,1)} %bitcast.17, bf16[4,80,256]{2,1,0:T(8,128)(2,1)} %pad_maximum_fusion.yt_ref, bf16[256,2048]{1,0:T(8,128)(2,1)} %w_ref.1, f32[1,2048]{1,0:T(1,128)} %bitcast.19, f32[1,2048]{1,0:T(1,128)} %bitcast.18), custom_call_target="tpu_custom_call" | custom-call | tf_op jit(solution)/shard_map/pallas_call | solution.py:436
  103.6 2.0 %copy.8 = f32[1,512,256]{2,1,0:T(8,128)} copy(f32[1,512,256]{1,2,0:T(8,128)} %bitcast.15) | data formatting | bytes 1048576 | tf_op jit(solution)/shard_map/broadcast_in_dim | solution.py:446
  (2 shorter events, 0.0 us)
Async XLA Ops:
  0.0 0.7 copy-start
  0.7 0.7 copy-start.1

commit v2 on v1

--- a/solution.py
+++ b/solution.py
@@ -106,14 +106,14 @@
 MESH = pl.DeviceIdType.MESH
 MASK_ROWS = 16
 COS = (
-    1.0,
-    -19.73920440673828,
-    64.93911743164062,
-    -85.45011138916016,
-    60.16743087768555,
-    -25.96688461303711,
-    6.527706146240234,
+    0.9999992251396179,
+    -19.738977432250977,
+    64.9285888671875,
+    -85.27084350585938,
+    58.78694152832031,
+    -21.0654296875,
 )
+ROUNDER = 1.5 * 2.0**23
 NT = (((1,), (1,)), ((), ()))
 
 
@@ -132,15 +132,17 @@
 
 def kernel(
     X, Z, chunk, entries,
-    sig_ref, yt_ref, w_ref, sc_ref, ph_ref, out_ref,
+    counts_ref, sig_ref, y_ref, w_ref, ids_ref, phases_ref, out_ref,
+    yt_own, sc_ref, ph_ref,
     sig_all, yt_all, hi, lo, proj, lhs, msk, vec, coef, vs, ust, own, got, totals, got_totals,
     scal, last, outbox, landing,
-    gs_send, gs_recv, gy_send, gy_recv, ex_send, ex_recv, t_send, t_recv,
+    gs_send, gs_recv, gy_send, gy_recv, fs_send, fs_recv, fy_send, fy_recv,
+    ex_send, ex_recv, t_send, t_recv,
     sc_send, sc_recv, la_send, la_recv, o_send, o_recv,
 ):
     rows, K = sig_ref.shape
     F = w_ref.shape[1]
-    cols = yt_ref.shape[1] - MASK_ROWS
+    cols = y_ref.shape[1] // Z
     C = 2 * cols
     B = X * Z
     n = B * rows
@@ -150,52 +152,90 @@
     z = lax.axis_index("asset")
     x = epoch // 2
     core = epoch % 2
-    mate = 2 * x + (1 - core)
 
     def at(xx, cc, zz):
         return {"epoch": 2 * xx + cc, "asset": zz}
 
+    def signal(peer):
+        pl.semaphore_signal(barrier, inc=1, device_id=peer, device_id_type=MESH)
+
     barrier = pltpu.get_barrier_semaphore()
-    peers = []
-    for d in range(1, B):
-        peers.append(at(lax.rem(x + d // Z, X), core, lax.rem(z + d % Z, Z)))
+    for d in range(1, Z):
+        signal(at(x, core, lax.rem(z + d, Z)))
     for d in range(Z):
-        peers.append(at(x, 1 - core, lax.rem(z + d, Z)))
-    for peer in peers:
-        pl.semaphore_signal(barrier, inc=1, device_id=peer, device_id_type=MESH)
-    pl.semaphore_wait(barrier, len(peers))
+        signal(at(x, 1 - core, lax.rem(z + d, Z)))
+
+    beside = sorted({1 % X, X - 1} - {0})
+    for d in beside:
+        signal(at(lax.rem(x + d, X), core, z))
+
+    count_here = counts_ref[0, 0]
+    alive = lax.broadcasted_iota(jnp.int32, (rows, 1), 0) < count_here
+    y = jnp.where(alive, y_ref[...].astype(f32), 0.0).T
+    alive = lax.broadcasted_iota(jnp.int32, (MASK_ROWS, rows), 1) < count_here
+    mask = jnp.where(alive, 1.0, 0.0).astype(jnp.bfloat16)
+    for b in range(Z):
+        yt_own[b, 0:cols, :] = y[b * cols:(b + 1) * cols].astype(jnp.bfloat16)
+        yt_own[b, cols:cols + MASK_ROWS, :] = mask
+    turn = 1.0 / (2.0 * math.pi)
+    sc_ref[...] = feature_scale(ids_ref[...]) * turn
+    ph_ref[...] = phases_ref[...] * turn - 0.25
+
+    pl.semaphore_wait(barrier, 2 * Z - 1 + len(beside))
 
     mine = x * Z + z
 
-    def sig_copy(d):
-        xx, zz = lax.rem(x + d // Z, X), lax.rem(z + d % Z, Z)
-        return pltpu.make_async_remote_copy(
-            src_ref=sig_ref, dst_ref=sig_all.at[mine],
-            send_sem=gs_send.at[d], recv_sem=gs_recv.at[d],
-            device_id=at(xx, core, zz), device_id_type=MESH)
-
-    def y_copy(d):
-        xx, zz = lax.rem(x + d // Z, X), lax.rem(z + d % Z, Z)
-        return pltpu.make_async_remote_copy(
-            src_ref=yt_ref.at[zz], dst_ref=yt_all.at[mine],
-            send_sem=gy_send.at[d], recv_sem=gy_recv.at[d],
-            device_id=at(xx, core, zz), device_id_type=MESH)
-
-    for d in range(1, B):
-        sig_copy(d).start()
-        y_copy(d).start()
+    def along(d):
+        zz = lax.rem(z + d, Z)
+        return (
+            pltpu.make_async_remote_copy(
+                src_ref=sig_ref, dst_ref=sig_all.at[mine],
+                send_sem=gs_send.at[d], recv_sem=gs_recv.at[d],
+                device_id=at(x, core, zz), device_id_type=MESH),
+            pltpu.make_async_remote_copy(
+                src_ref=yt_own.at[zz], dst_ref=yt_all.at[mine],
+                send_sem=gy_send.at[d], recv_sem=gy_recv.at[d],
+                device_id=at(x, core, zz), device_id_type=MESH),
+        )
+
+    def upward(slot):
+        return (
+            pltpu.make_async_remote_copy(
+                src_ref=sig_all.at[slot], dst_ref=sig_all.at[slot],
+                send_sem=fs_send.at[slot], recv_sem=fs_recv.at[slot],
+                device_id=at(x + 1, core, z), device_id_type=MESH),
+            pltpu.make_async_remote_copy(
+                src_ref=yt_all.at[slot], dst_ref=yt_all.at[slot],
+                send_sem=fy_send.at[slot], recv_sem=fy_recv.at[slot],
+                device_id=at(x + 1, core, z), device_id_type=MESH),
+        )
+
+    for d in range(1, Z):
+        for copy in along(d):
+            copy.start()
     sig_all[mine] = sig_ref[...]
-    yt_all[mine] = yt_ref[z]
-
-    def block(d, carry):
-        @pl.when(d > 0)
+    yt_all[mine] = yt_own[z]
+
+    def block(dz, dx):
+        xx = x - dx
+        zz = lax.rem(z + Z - dz, Z)
+        slot = xx * Z + zz
+
+        @pl.when((dx == 0) & (dz > 0))
         def _():
-            sig_copy(d).wait()
-            y_copy(d).wait()
-
-        xx = lax.rem(x + X - d // Z, X)
-        zz = lax.rem(z + Z - lax.rem(d, Z), Z)
-        slot = xx * Z + zz
+            for copy in along(dz):
+                copy.wait()
+
+        @pl.when(dx > 0)
+        def _():
+            for copy in upward(slot):
+                copy.wait_recv()
+
+        @pl.when(x < X - 1)
+        def _():
+            for copy in upward(slot):
+                copy.start()
+
         base = pl.multiple_of(slot * rows, rows)
         live = yt_all[slot, cols:cols + MASK_ROWS, :].astype(f32)[0:1, :]
         y = yt_all[slot, 0:cols, :].astype(f32)
@@ -214,7 +254,7 @@
             def strip(r, carry):
                 r0 = pl.multiple_of(r * 16, 16)
                 t = proj[pl.ds(r0, 16), part] * scale + phase
-                f = t - jnp.round(t)
+                f = t - ((t + ROUNDER) - ROUNDER)
                 s = f * f
                 acc = s * COS[-1] + COS[-2]
                 for c in COS[-3::-1]:
@@ -226,9 +266,34 @@
                 return carry
 
             lax.fori_loop(0, rows // 16, strip, 0, unroll=4)
+
+    def column(dz, carry):
+        def one(dx, carry):
+            block(dz, dx)
+            return carry
+
+        return lax.fori_loop(0, x + 1, one, carry)
+
+    lax.fori_loop(0, Z, column, 0)
+
+    def absent(slot, carry):
+        here = pl.ds(pl.multiple_of(slot * rows, rows), rows)
+        hi[here, :] = jnp.zeros((rows, F), jnp.bfloat16)
+        lo[here, :] = jnp.zeros((rows, F), jnp.bfloat16)
+        msk[:, :, here] = jnp.zeros((2, 8, rows), f32)
+        lhs[:, here] = jnp.zeros((C, rows), jnp.bfloat16)
         return carry
 
-    lax.fori_loop(0, B, block, 0)
+    lax.fori_loop((x + 1) * Z, B, absent, 0)
+
+    @pl.when(x < X - 1)
+    def _():
+        def sent(slot, carry):
+            for copy in upward(slot):
+                copy.wait_send()
+            return carry
+
+        lax.fori_loop(0, (x + 1) * Z, sent, 0)
 
     is_first = lax.broadcasted_iota(jnp.int32, (C, 1), 0) < cols
 
@@ -287,8 +352,11 @@
         def forward(j, total):
             base = pl.multiple_of(j * rows, rows)
             here = pl.ds(base, rows)
-            u = mm_nt(vs[...], hi[here, :])
-            u = u[0:C] + u[C:] + mm_nt(vs[0:C, :], lo[here, :])
+            if final:
+                u = mm_nt(vs[0:C, :], hi[here, :])
+            else:
+                u = mm_nt(vs[...], hi[here, :])
+                u = u[0:C] + u[C:]
             u = jnp.concatenate(
                 [u[0:cols] * msk[0, 0:1, here], u[cols:] * msk[1, 0:1, here]], axis=0)
             if final:
@@ -380,7 +448,7 @@
     landing[z] = outbox[z]
     for copy in copies:
         copy.wait()
-    out_ref[...] = landing[...].reshape(Z * cols, width)
+    out_ref[...] = landing[...].reshape(Z * cols, width).T
 
 
 def scratch_of(X, Z, rows, K, F, cols, chunk):
@@ -390,6 +458,7 @@
     nch = F // chunk
     f32, bf16 = jnp.float32, jnp.bfloat16
     buffers = [
+        ((Z, cols + MASK_ROWS, rows), bf16), ((1, F), f32), ((1, F), f32),
         ((B, rows, K), bf16), ((B, cols + MASK_ROWS, rows), bf16),
         ((n, F), bf16), ((n, F), bf16), ((max(rows, C), F), f32), ((C, n), bf16),
         ((2, 8, n), f32), ((C, F), f32), ((C, F), f32), ((2 * C, F), bf16), ((2 * C, n), bf16),
@@ -399,7 +468,7 @@
         ((Z, cols, F // Z), f32), ((Z, cols, F // Z), f32),
     ]
     held = sum(math.prod(shape) * jnp.dtype(dtype).itemsize for shape, dtype in buffers)
-    sems = [(B,)] * 4 + [(ITERS, nch)] * 2 + [()] * 2 + [(ITERS, Z)] * 2 + [(2 * Z,)] * 2 + [(Z,)] * 2
+    sems = [(Z,)] * 4 + [(B,)] * 4 + [(ITERS, nch)] * 2 + [()] * 2 + [(ITERS, Z)] * 2 + [(2 * Z,)] * 2 + [(Z,)] * 2
     return buffers, sems, held
 
 
@@ -424,26 +493,18 @@
     F = feature_weights.shape[1]
     T = targets.shape[2]
     cols, chunk, buffers, sems = plan(E, Z, rows, K, F, T)
-    live = jnp.arange(rows) < row_counts[0, 0]
-    returns = jnp.where(live[:, None], targets[0], jnp.zeros((), targets.dtype)).T
-    returns = returns.reshape(Z, cols, rows)
-    mask = jnp.broadcast_to(live.astype(targets.dtype), (Z, MASK_ROWS, rows))
-    returns = jnp.concatenate([returns, mask], axis=1)
-    turn = 1.0 / (2.0 * math.pi)
-    scale = (feature_scale(spread_ids) * turn)[None, :]
-    phase = (phases * turn - 0.25)[None, :]
     vmem = pl.BlockSpec(memory_space=pltpu.VMEM)
     out = pl.pallas_call(
         functools.partial(kernel, E // 2, Z, chunk, float(F * T)),
-        out_shape=jax.ShapeDtypeStruct((T, F // Z), jnp.float32),
-        in_specs=[vmem] * 5,
+        out_shape=jax.ShapeDtypeStruct((F // Z, T), jnp.float32),
+        in_specs=[pl.BlockSpec(memory_space=pltpu.SMEM)] + [vmem] * 5,
         out_specs=vmem,
         scratch_shapes=[pltpu.VMEM(s, d) for s, d in buffers]
         + [pltpu.SemaphoreType.DMA(s) if s else pltpu.SemaphoreType.DMA for s in sems],
         compiler_params=pltpu.CompilerParams(
             collective_id=0, has_side_effects=True, vmem_limit_bytes=56 * 2**20),
-    )(signals[0], returns, feature_weights, scale, phase)
-    return out.T[None]
+    )(row_counts, signals[0], targets[0], feature_weights, spread_ids[None, :], phases[None, :])
+    return out[None]
 
 
 def solution(mesh):

time: 108 us -> 89.2 us (0.83); the launches traced: 106 us -> 89 us
  Pallas kernels: 99.8 us -> 86.4 us
  other arithmetic: 2.88 us -> 0 us
    pallas_call x1, Pallas kernels: 99.8 us -> 86.4 us  [fused(): pl.pallas_call(functools.partial(kernel, E // 2, Z, chunk, float(F * T)),...]
    broadcast_in_dim x2 -> x0, local copies, waits for them, and re-layouts: 2.04 us -> none  [the longest x1 2.04 us: fused(): return out.T[None]]
    unnamed x4 -> x1, local copies, waits for them, and re-layouts: 0.12 us -> 1.87 us
where the time goes in v2:
time: 89.2 us; the launch traced here: 89 us
  Pallas kernels  86.4 us (97%)
  local copies, waits for them, and re-layouts  1.87 us (2%)
    pallas_call x1, Pallas kernels, fused(): pl.pallas_call(functools.partial(kernel, E // 2, Z, chunk, float(F * T)),...  86.4 us
    unnamed x1, local copies, waits for them, and re-layouts  1.87 us

profile of v2, /device:TPU:11, one launch (start us, length us, event | category | flops | bytes accessed | tf_op | source)
XLA Modules:
  0.0 89.0 jit_solution(17134796869250639239)
XLA Ops:
  0.7 86.4 %shard_map.64 = f32[512,256]{1,0:T(8,128)} custom-call(s32[1,1]{1,0:T(1,128)S(6)} %copy.8.counts_ref, bf16[256,256]{1,0:T(8,128)(2,1)} %bitcast.6, bf16[256,256]{1,0:T(8,128)(2,1)} %bitcast.7, bf16[256,2048]{1,0:T(8,128)(2,1)} %w_ref.1, s32[1,2048]{1,0:T(1,128)} %bitcast.8, f32[1,2048]{1,0:T(1,128)} %bitcast.9), custom_call_target="tpu_custom_call" | custom-call | tf_op jit(solution)/shard_map/pallas_call | solution.py:497
  87.1 1.9 %copy.9 = f32[1,512,256]{2,1,0:T(8,128)} copy(f32[1,512,256]{2,1,0:T(8,128)} %bitcast.5) | data formatting | bytes 1048576

commit v3 on v2

--- a/solution.py
+++ b/solution.py
@@ -114,15 +114,8 @@
     -21.0654296875,
 )
 ROUNDER = 1.5 * 2.0**23
-NT = (((1,), (1,)), ((), ()))
-
-
 def mm(a, b):
     return jnp.dot(a, b, preferred_element_type=jnp.float32)
-
-
-def mm_nt(a, b):
-    return lax.dot_general(a, b, NT, preferred_element_type=jnp.float32)
 
 
 def split(a):
@@ -147,6 +140,7 @@
     B = X * Z
     n = B * rows
     nch = F // chunk
+    band = 2 * rows
     f32 = jnp.float32
     epoch = lax.axis_index("epoch")
     z = lax.axis_index("asset")
@@ -242,7 +236,7 @@
         for q in range(2):
             allow = jnp.where(2 * xx + core <= 2 * x + q, 1.0, 0.0).astype(f32)
             msk[q, :, pl.ds(base, rows)] = jnp.broadcast_to(live * allow, (8, rows))
-            lhs[q * cols:(q + 1) * cols, pl.ds(base, rows)] = (y * allow).astype(jnp.bfloat16)
+            lhs[q * cols:(q + 1) * cols, :] = (y * allow).astype(jnp.bfloat16)
         for k in range(nch):
             part = slice(k * chunk, (k + 1) * chunk)
             proj[:, part] = mm(sig_all[slot], w_ref[:, part])
@@ -266,6 +260,10 @@
                 return carry
 
             lax.fori_loop(0, rows // 16, strip, 0, unroll=4)
+            here = pl.ds(base, rows)
+            vec[:, part] += mm(lhs[...], hi[here, part]) + mm(lhs[...], lo[here, part])
+
+    vec[...] = jnp.zeros_like(vec)
 
     def column(dz, carry):
         def one(dx, carry):
@@ -281,7 +279,6 @@
         hi[here, :] = jnp.zeros((rows, F), jnp.bfloat16)
         lo[here, :] = jnp.zeros((rows, F), jnp.bfloat16)
         msk[:, :, here] = jnp.zeros((2, 8, rows), f32)
-        lhs[:, here] = jnp.zeros((C, rows), jnp.bfloat16)
         return carry
 
     lax.fori_loop((x + 1) * Z, B, absent, 0)
@@ -316,11 +313,16 @@
 
     for k in range(nch):
         part = slice(k * chunk, (k + 1) * chunk)
-        own[0, k] = mm(lhs[...], hi[:, part]) + mm(lhs[...], lo[:, part])
+        own[0, k] = vec[:, part]
         exchange(0, k).start()
     count_copy.wait()
     count = [totals[q][0:1, 0:1] + got_totals[q][0:1, 0:1] for q in range(2)]
     inverse = spread(1.0 / count[0], 1.0 / count[1])
+
+    def keep(v, part):
+        high, low = split(v.T)
+        vs[part, 0:C] = high
+        vs[part, C:2 * C] = low
 
     norm = jnp.zeros((C, 1), f32)
     for k in range(nch):
@@ -328,9 +330,7 @@
         exchange(0, k).wait()
         v = (own[0, k] + got[0, k]) * inverse
         vec[:, part] = v
-        high, low = split(v)
-        vs[0:C, part] = high
-        vs[C:2 * C, part] = low
+        keep(v, part)
         norm = norm + jnp.sum(v * v, axis=1, keepdims=True)
 
     tile_row = lax.broadcasted_iota(jnp.int32, (8, 128), 0)
@@ -350,13 +350,13 @@
         final = it == ITERS - 1
 
         def forward(j, total):
-            base = pl.multiple_of(j * rows, rows)
-            here = pl.ds(base, rows)
+            base = pl.multiple_of(j * band, band)
+            here = pl.ds(base, band)
             if final:
-                u = mm_nt(vs[0:C, :], hi[here, :])
+                u = mm(hi[here, :], vs[:, 0:C]).T
             else:
-                u = mm_nt(vs[...], hi[here, :])
-                u = u[0:C] + u[C:]
+                u = mm(hi[here, :], vs[...])
+                u = (u[:, 0:C] + u[:, C:]).T
             u = jnp.concatenate(
                 [u[0:cols] * msk[0, 0:1, here], u[cols:] * msk[1, 0:1, here]], axis=0)
             if final:
@@ -366,7 +366,7 @@
             ust[C:2 * C, here] = low
             return total
 
-        square = lax.fori_loop(0, B, forward, jnp.zeros((C, 1), f32))
+        square = lax.fori_loop(0, n // band, forward, jnp.zeros((C, 1), f32))
         if final:
             last[core * Z + z] = tile(norm, square)
             copies = []
@@ -427,9 +427,7 @@
                 coef[:, part] = step * v if it == 0 else coef[:, part] + step * v
                 v = v - step * proj[0:C, part]
                 vec[:, part] = v
-                high, low = split(v)
-                vs[0:C, part] = high
-                vs[C:2 * C, part] = low
+                keep(v, part)
                 norm = norm + jnp.sum(v * v, axis=1, keepdims=True)
 
     width = F // Z
@@ -460,8 +458,8 @@
     buffers = [
         ((Z, cols + MASK_ROWS, rows), bf16), ((1, F), f32), ((1, F), f32),
         ((B, rows, K), bf16), ((B, cols + MASK_ROWS, rows), bf16),
-        ((n, F), bf16), ((n, F), bf16), ((max(rows, C), F), f32), ((C, n), bf16),
-        ((2, 8, n), f32), ((C, F), f32), ((C, F), f32), ((2 * C, F), bf16), ((2 * C, n), bf16),
+        ((n, F), bf16), ((n, F), bf16), ((max(rows, C), F), f32), ((C, rows), bf16),
+        ((2, 8, n), f32), ((C, F), f32), ((C, F), f32), ((F, 2 * C), bf16), ((2 * C, n), bf16),
         ((ITERS, nch, C, chunk), f32), ((ITERS, nch, C, chunk), f32),
         ((2, 8, 128), f32), ((2, 8, 128), f32),
         ((ITERS, Z, 8, 128), f32), ((2 * Z, 8, 128), f32),
@@ -479,7 +477,7 @@
     if E % 2 or T % Z or F % Z:
         return None
     cols, chunk = T // Z, 512
-    if cols % 16 or rows % 128 or F % chunk or (F // Z) % 128 or K % 128:
+    if (E // 2 * Z) % 2 or cols % 16 or rows % 128 or F % chunk or (F // Z) % 128 or K % 128:
         return None
     buffers, sems, held = scratch_of(E // 2, Z, rows, K, F, cols, chunk)
     if held > VMEM_BUDGET:

time: 89.2 us -> 87.8 us (0.984)
  Pallas kernels: 86.4 us -> 85.1 us
    pallas_call x1, Pallas kernels: 86.4 us -> 85.1 us  [fused(): pl.pallas_call(functools.partial(kernel, E // 2, Z, chunk, float(F * T)),...]
where the time goes in v3:
time: 87.8 us; the launch traced here: 87.6 us
  Pallas kernels  85.1 us (97%)
  local copies, waits for them, and re-layouts  1.87 us (2%)
    pallas_call x1, Pallas kernels, fused(): pl.pallas_call(functools.partial(kernel, E // 2, Z, chunk, float(F * T)),...  85.1 us
    unnamed x1, local copies, waits for them, and re-layouts  1.87 us

profile of v3, /device:TPU:11, one launch (start us, length us, event | category | flops | bytes accessed | tf_op | source)
XLA Modules:
  0.0 87.6 jit_solution(11069563656733121573)
XLA Ops:
  0.7 85.1 %shard_map.64 = f32[512,256]{1,0:T(8,128)} custom-call(s32[1,1]{1,0:T(1,128)S(6)} %copy.8.counts_ref, bf16[256,256]{1,0:T(8,128)(2,1)} %bitcast.6, bf16[256,256]{1,0:T(8,128)(2,1)} %bitcast.7, bf16[256,2048]{1,0:T(8,128)(2,1)} %w_ref.1, s32[1,2048]{1,0:T(1,128)} %bitcast.8, f32[1,2048]{1,0:T(1,128)} %bitcast.9), custom_call_target="tpu_custom_call" | custom-call | tf_op jit(solution)/shard_map/pallas_call | solution.py:495
  85.7 1.9 %copy.9 = f32[1,512,256]{2,1,0:T(8,128)} copy(f32[1,512,256]{2,1,0:T(8,128)} %bitcast.5) | data formatting | bytes 1048576

commit v4 on v3

--- a/solution.py
+++ b/solution.py
@@ -127,7 +127,7 @@
     X, Z, chunk, entries,
     counts_ref, sig_ref, y_ref, w_ref, ids_ref, phases_ref, out_ref,
     yt_own, sc_ref, ph_ref,
-    sig_all, yt_all, hi, lo, proj, lhs, msk, vec, coef, vs, ust, own, got, totals, got_totals,
+    sig_all, yt_all, hi, lo, proj, lhs, msk, vec, res, u_now, u_image, vs, ust, own, got, totals, got_totals,
     scal, last, outbox, landing,
     gs_send, gs_recv, gy_send, gy_recv, fs_send, fs_recv, fy_send, fy_recv,
     ex_send, ex_recv, t_send, t_recv,
@@ -210,6 +210,17 @@
     sig_all[mine] = sig_ref[...]
     yt_all[mine] = yt_own[z]
 
+    is_first = lax.broadcasted_iota(jnp.int32, (C, 1), 0) < cols
+
+    def spread(a0, a1):
+        return jnp.where(is_first, a0, a1)
+
+    def exchange(s, k):
+        return pltpu.make_async_remote_copy(
+            src_ref=own.at[s, k], dst_ref=got.at[s, k],
+            send_sem=ex_send.at[s, k], recv_sem=ex_recv.at[s, k],
+            device_id=at(x, 1 - core, z), device_id_type=MESH)
+
     def block(dz, dx):
         xx = x - dx
         zz = lax.rem(z + Z - dz, Z)
@@ -261,9 +272,13 @@
 
             lax.fori_loop(0, rows // 16, strip, 0, unroll=4)
             here = pl.ds(base, rows)
-            vec[:, part] += mm(lhs[...], hi[here, part]) + mm(lhs[...], lo[here, part])
-
-    vec[...] = jnp.zeros_like(vec)
+            own[0, k] += mm(lhs[...], hi[here, part]) + mm(lhs[...], lo[here, part])
+
+            @pl.when((dz == Z - 1) & (dx == x))
+            def _():
+                exchange(0, k).start()
+
+    own[0] = jnp.zeros((nch, C, chunk), f32)
 
     def column(dz, carry):
         def one(dx, carry):
@@ -292,46 +307,59 @@
 
         lax.fori_loop(0, (x + 1) * Z, sent, 0)
 
-    is_first = lax.broadcasted_iota(jnp.int32, (C, 1), 0) < cols
-
-    def spread(a0, a1):
-        return jnp.where(is_first, a0, a1)
-
-    totals[...] = jnp.zeros_like(totals)
     for q in range(2):
         totals[q] = jnp.broadcast_to(jnp.sum(msk[q], axis=1, keepdims=True), totals.shape[1:])
     count_copy = pltpu.make_async_remote_copy(
         src_ref=totals, dst_ref=got_totals, send_sem=t_send, recv_sem=t_recv,
         device_id=at(x, 1 - core, z), device_id_type=MESH)
     count_copy.start()
-
-    def exchange(s, k):
-        return pltpu.make_async_remote_copy(
-            src_ref=own.at[s, k], dst_ref=got.at[s, k],
-            send_sem=ex_send.at[s, k], recv_sem=ex_recv.at[s, k],
-            device_id=at(x, 1 - core, z), device_id_type=MESH)
-
-    for k in range(nch):
-        part = slice(k * chunk, (k + 1) * chunk)
-        own[0, k] = vec[:, part]
-        exchange(0, k).start()
     count_copy.wait()
     count = [totals[q][0:1, 0:1] + got_totals[q][0:1, 0:1] for q in range(2)]
     inverse = spread(1.0 / count[0], 1.0 / count[1])
+
+    width = F // Z
+    first = pl.multiple_of(core * cols, cols)
+
+    def piece(s, d):
+        zz = lax.rem(z + d, Z)
+        columns = pl.ds(pl.multiple_of(zz * width, width), width)
+        return pltpu.make_async_remote_copy(
+            src_ref=vec.at[s, pl.ds(first, cols), columns], dst_ref=landing.at[s, z],
+            send_sem=o_send.at[s, d], recv_sem=o_recv.at[s, d],
+            device_id=at(x, core, zz), device_id_type=MESH)
+
+    def send_pieces(s):
+        for d in range(1, Z):
+            piece(s, d).start()
+        columns = pl.ds(pl.multiple_of(z * width, width), width)
+        landing[s, z] = vec[s, pl.ds(first, cols), columns]
 
     def keep(v, part):
         high, low = split(v.T)
         vs[part, 0:C] = high
         vs[part, C:2 * C] = low
+
+    def forward(to):
+        def one(j, carry):
+            here = pl.ds(pl.multiple_of(j * band, band), band)
+            u = mm(hi[here, :], vs[...])
+            u = (u[:, 0:C] + u[:, C:]).T
+            to[0:cols, here] = u[0:cols] * msk[0, 0:1, here]
+            to[cols:C, here] = u[cols:] * msk[1, 0:1, here]
+            return carry
+
+        lax.fori_loop(0, n // band, one, 0)
 
     norm = jnp.zeros((C, 1), f32)
     for k in range(nch):
         part = slice(k * chunk, (k + 1) * chunk)
         exchange(0, k).wait()
         v = (own[0, k] + got[0, k]) * inverse
-        vec[:, part] = v
+        vec[0, :, part] = v
         keep(v, part)
         norm = norm + jnp.sum(v * v, axis=1, keepdims=True)
+    send_pieces(0)
+    forward(u_now)
 
     tile_row = lax.broadcasted_iota(jnp.int32, (8, 128), 0)
 
@@ -341,112 +369,94 @@
             out = jnp.where(tile_row == i, jnp.sum(a, axis=0, keepdims=True), out)
         return out
 
-    def step_of(a):
+    steps = []
+    for it in range(ITERS - 1):
+        s = it + 1
+        for k in range(n // chunk):
+            part = slice(k * chunk, (k + 1) * chunk)
+            high, low = split(u_now[:, part])
+            ust[0:C, part] = high
+            ust[C:2 * C, part] = low
+        for k in range(nch):
+            part = slice(k * chunk, (k + 1) * chunk)
+            image = mm(ust[...], hi[:, part])
+            own[s, k] = image[0:C] + image[C:] + mm(ust[0:C, :], lo[:, part])
+            exchange(s, k).start()
+        curve = jnp.zeros((C, 1), f32)
+        for k in range(nch):
+            part = slice(k * chunk, (k + 1) * chunk)
+            exchange(s, k).wait()
+            v = res[:, part] if it else vec[0, :, part]
+            image = (own[s, k] + got[s, k]) * inverse + ridge_penalty * v
+            vec[s, :, part] = image
+            keep(image, part)
+            curve = curve + jnp.sum(v * image, axis=1, keepdims=True)
+        scal[it, z] = tile(norm, curve)
+        copies = []
+        for d in range(1, Z):
+            copies.append(pltpu.make_async_remote_copy(
+                src_ref=scal.at[it, z], dst_ref=scal.at[it, z],
+                send_sem=sc_send.at[it, d], recv_sem=sc_recv.at[it, d],
+                device_id=at(x, core, lax.rem(z + d, Z)), device_id_type=MESH))
+        for copy in copies:
+            copy.start()
+        send_pieces(s)
+        forward(u_image)
+        for copy in copies:
+            copy.wait()
+        a = scal[it, 0]
+        for i in range(1, Z):
+            a = a + scal[it, i]
         res_norm = spread(a[0:1, 0:1], a[1:2, 0:1])
         res_curve = spread(a[2:3, 0:1], a[3:4, 0:1])
-        return res_norm / entries / (res_curve / entries + epsilon)
-
-    for it in range(ITERS):
-        final = it == ITERS - 1
-
-        def forward(j, total):
-            base = pl.multiple_of(j * band, band)
-            here = pl.ds(base, band)
-            if final:
-                u = mm(hi[here, :], vs[:, 0:C]).T
-            else:
-                u = mm(hi[here, :], vs[...])
-                u = (u[:, 0:C] + u[:, C:]).T
-            u = jnp.concatenate(
-                [u[0:cols] * msk[0, 0:1, here], u[cols:] * msk[1, 0:1, here]], axis=0)
-            if final:
-                return total + jnp.sum(u * u, axis=1, keepdims=True)
-            high, low = split(u)
-            ust[0:C, here] = high
-            ust[C:2 * C, here] = low
-            return total
-
-        square = lax.fori_loop(0, n // band, forward, jnp.zeros((C, 1), f32))
-        if final:
-            last[core * Z + z] = tile(norm, square)
-            copies = []
-            for d in range(1, 2 * Z):
-                cc, zz = lax.rem(core + d // Z, 2), lax.rem(z + d % Z, Z)
-                copies.append(pltpu.make_async_remote_copy(
-                    src_ref=last.at[core * Z + z], dst_ref=last.at[core * Z + z],
-                    send_sem=la_send.at[d], recv_sem=la_recv.at[d],
-                    device_id=at(x, cc, zz), device_id_type=MESH))
-            for copy in copies:
-                copy.start()
-            for copy in copies:
-                copy.wait()
-            a = last[0]
-            for i in range(1, 2 * Z):
-                a = a + last[i]
-            norms = spread(a[0:1, 0:1], a[1:2, 0:1]) * 0.5
-            curve = spread(a[2:3, 0:1] / count[0], a[3:4, 0:1] / count[1]) + ridge_penalty * norms
-            step = norms / entries / (curve / entries + epsilon)
-            root = spread(jnp.sqrt(count[0]), jnp.sqrt(count[1]))
-            for k in range(nch):
-                part = slice(k * chunk, (k + 1) * chunk)
-                coef[:, part] = (coef[:, part] + step * vec[:, part]) * root
-        else:
-            s = it + 1
-            for k in range(nch):
-                part = slice(k * chunk, (k + 1) * chunk)
-                image = mm(ust[...], hi[:, part])
-                own[s, k] = image[0:C] + image[C:] + mm(ust[0:C, :], lo[:, part])
-                exchange(s, k).start()
-            curve = jnp.zeros((C, 1), f32)
-            for k in range(nch):
-                part = slice(k * chunk, (k + 1) * chunk)
-                exchange(s, k).wait()
-                v = vec[:, part]
-                image = (own[s, k] + got[s, k]) * inverse + ridge_penalty * v
-                proj[0:C, part] = image
-                curve = curve + jnp.sum(v * image, axis=1, keepdims=True)
-            scal[it, z] = tile(norm, curve)
-            copies = []
-            for d in range(1, Z):
-                copies.append(pltpu.make_async_remote_copy(
-                    src_ref=scal.at[it, z], dst_ref=scal.at[it, z],
-                    send_sem=sc_send.at[it, d], recv_sem=sc_recv.at[it, d],
-                    device_id=at(x, core, lax.rem(z + d, Z)), device_id_type=MESH))
-            for copy in copies:
-                copy.start()
-            for copy in copies:
-                copy.wait()
-            a = scal[it, 0]
-            for i in range(1, Z):
-                a = a + scal[it, i]
-            step = step_of(a)
-            norm = jnp.zeros((C, 1), f32)
-            for k in range(nch):
-                part = slice(k * chunk, (k + 1) * chunk)
-                v = vec[:, part]
-                coef[:, part] = step * v if it == 0 else coef[:, part] + step * v
-                v = v - step * proj[0:C, part]
-                vec[:, part] = v
-                keep(v, part)
-                norm = norm + jnp.sum(v * v, axis=1, keepdims=True)
-
-    width = F // Z
-    first = pl.multiple_of(core * cols, cols)
-    for b in range(Z):
-        outbox[b] = coef[pl.ds(first, cols), b * width:(b + 1) * width]
+        step = res_norm / entries / (res_curve / entries + epsilon)
+        steps.append(step)
+        norm = jnp.zeros((C, 1), f32)
+        for k in range(nch):
+            part = slice(k * chunk, (k + 1) * chunk)
+            v = res[:, part] if it else vec[0, :, part]
+            v = v - step * vec[s, :, part]
+            res[:, part] = v
+            norm = norm + jnp.sum(v * v, axis=1, keepdims=True)
+        square = jnp.zeros((C, 1), f32)
+        for k in range(n // chunk):
+            part = slice(k * chunk, (k + 1) * chunk)
+            u = u_now[:, part] - step * u_image[:, part]
+            u_now[:, part] = u
+            square = square + jnp.sum(u * u, axis=1, keepdims=True)
+
+    last[core * Z + z] = tile(norm, square)
     copies = []
-    for d in range(1, Z):
-        zz = lax.rem(z + d, Z)
+    for d in range(1, 2 * Z):
+        cc, zz = lax.rem(core + d // Z, 2), lax.rem(z + d % Z, Z)
         copies.append(pltpu.make_async_remote_copy(
-            src_ref=outbox.at[zz], dst_ref=landing.at[z],
-            send_sem=o_send.at[d], recv_sem=o_recv.at[d],
-            device_id=at(x, core, zz), device_id_type=MESH))
+            src_ref=last.at[core * Z + z], dst_ref=last.at[core * Z + z],
+            send_sem=la_send.at[d], recv_sem=la_recv.at[d],
+            device_id=at(x, cc, zz), device_id_type=MESH))
     for copy in copies:
         copy.start()
-    landing[z] = outbox[z]
     for copy in copies:
         copy.wait()
-    out_ref[...] = landing[...].reshape(Z * cols, width).T
+    a = last[0]
+    for i in range(1, 2 * Z):
+        a = a + last[i]
+    norms = spread(a[0:1, 0:1], a[1:2, 0:1]) * 0.5
+    curve = spread(a[2:3, 0:1] / count[0], a[3:4, 0:1] / count[1]) + ridge_penalty * norms
+    steps.append(norms / entries / (curve / entries + epsilon))
+
+    def here_of(column):
+        return jnp.where(core == 0, column[0:1], column[cols:cols + 1])
+
+    root = here_of(spread(jnp.sqrt(count[0]), jnp.sqrt(count[1])))
+    s0, s1, s2 = [here_of(step) for step in steps]
+    for s in range(ITERS):
+        for d in range(1, Z):
+            piece(s, d).wait()
+    for i in range(Z):
+        coef = (s0 + s1 + s2) * landing[0, i] - (s1 + s2) * s0 * landing[1, i]
+        coef = coef - s1 * s2 * landing[2, i]
+        outbox[i * cols:(i + 1) * cols, :] = coef * root
+    out_ref[...] = outbox[...].T
 
 
 def scratch_of(X, Z, rows, K, F, cols, chunk):
@@ -458,15 +468,16 @@
     buffers = [
         ((Z, cols + MASK_ROWS, rows), bf16), ((1, F), f32), ((1, F), f32),
         ((B, rows, K), bf16), ((B, cols + MASK_ROWS, rows), bf16),
-        ((n, F), bf16), ((n, F), bf16), ((max(rows, C), F), f32), ((C, rows), bf16),
-        ((2, 8, n), f32), ((C, F), f32), ((C, F), f32), ((F, 2 * C), bf16), ((2 * C, n), bf16),
+        ((n, F), bf16), ((n, F), bf16), ((rows, F), f32), ((C, rows), bf16),
+        ((2, 8, n), f32), ((ITERS, C, F), f32), ((C, F), f32),
+        ((C, n), f32), ((C, n), f32), ((F, 2 * C), bf16), ((2 * C, n), bf16),
         ((ITERS, nch, C, chunk), f32), ((ITERS, nch, C, chunk), f32),
         ((2, 8, 128), f32), ((2, 8, 128), f32),
         ((ITERS, Z, 8, 128), f32), ((2 * Z, 8, 128), f32),
-        ((Z, cols, F // Z), f32), ((Z, cols, F // Z), f32),
+        ((Z * cols, F // Z), f32), ((ITERS, Z, cols, F // Z), f32),
     ]
     held = sum(math.prod(shape) * jnp.dtype(dtype).itemsize for shape, dtype in buffers)
-    sems = [(Z,)] * 4 + [(B,)] * 4 + [(ITERS, nch)] * 2 + [()] * 2 + [(ITERS, Z)] * 2 + [(2 * Z,)] * 2 + [(Z,)] * 2
+    sems = [(Z,)] * 4 + [(B,)] * 4 + [(ITERS, nch)] * 2 + [()] * 2 + [(ITERS, Z)] * 2 + [(2 * Z,)] * 2 + [(ITERS, Z)] * 2
     return buffers, sems, held
 
 
@@ -477,7 +488,8 @@
     if E % 2 or T % Z or F % Z:
         return None
     cols, chunk = T // Z, 512
-    if (E // 2 * Z) % 2 or cols % 16 or rows % 128 or F % chunk or (F // Z) % 128 or K % 128:
+    n_bad = (E // 2 * Z * rows) % chunk
+    if (E // 2 * Z) % 2 or ITERS != 3 or n_bad or cols % 16 or rows % 128 or F % chunk or (F // Z) % 128 or K % 128:
         return None
     buffers, sems, held = scratch_of(E // 2, Z, rows, K, F, cols, chunk)
     if held > VMEM_BUDGET:

time: 87.8 us -> 81.2 us (0.925); the launches traced: 87.6 us -> 80.1 us
  Pallas kernels: 85.1 us -> 77.5 us
    pallas_call x1, Pallas kernels: 85.1 us -> 77.5 us  [fused(): pl.pallas_call(functools.partial(kernel, E // 2, Z, chunk, float(F * T)),...]
where the time goes in v4:
time: 81.2 us; the launch traced here: 80.1 us
  Pallas kernels  77.5 us (95%)
  local copies, waits for them, and re-layouts  1.87 us (2%)
    pallas_call x1, Pallas kernels, fused(): pl.pallas_call(functools.partial(kernel, E // 2, Z, chunk, float(F * T)),...  77.5 us
    unnamed x1, local copies, waits for them, and re-layouts  1.87 us

profile of v4, /device:TPU:11, one launch (start us, length us, event | category | flops | bytes accessed | tf_op | source)
XLA Modules:
  0.0 80.1 jit_solution(16088672479854390574)
XLA Ops:
  0.7 77.5 %shard_map.64 = f32[512,256]{1,0:T(8,128)} custom-call(s32[1,1]{1,0:T(1,128)S(6)} %copy.8.counts_ref, bf16[256,256]{1,0:T(8,128)(2,1)} %bitcast.6, bf16[256,256]{1,0:T(8,128)(2,1)} %bitcast.7, bf16[256,2048]{1,0:T(8,128)(2,1)} %w_ref.1, s32[1,2048]{1,0:T(1,128)} %bitcast.8, f32[1,2048]{1,0:T(1,128)} %bitcast.9), custom_call_target="tpu_custom_call" | custom-call | tf_op jit(solution)/shard_map/pallas_call | solution.py:507
  78.2 1.9 %copy.9 = f32[1,512,256]{2,1,0:T(8,128)} copy(f32[1,512,256]{2,1,0:T(8,128)} %bitcast.5) | data formatting | bytes 1048576

commit v5 on v4

--- a/solution.py
+++ b/solution.py
@@ -179,18 +179,34 @@
 
     mine = x * Z + z
 
-    def along(d):
+    def hop(zz, way):
+        slot = x * Z + zz
+        return pltpu.make_async_remote_copy(
+            src_ref=sig_all.at[slot], dst_ref=sig_all.at[slot],
+            send_sem=gs_send.at[way, zz], recv_sem=gs_recv.at[zz],
+            device_id=at(x, core, lax.rem(z + 2 * way - 1 + Z, Z)), device_id_type=MESH)
+
+    def y_copy(d):
         zz = lax.rem(z + d, Z)
-        return (
-            pltpu.make_async_remote_copy(
-                src_ref=sig_ref, dst_ref=sig_all.at[mine],
-                send_sem=gs_send.at[d], recv_sem=gs_recv.at[d],
-                device_id=at(x, core, zz), device_id_type=MESH),
-            pltpu.make_async_remote_copy(
-                src_ref=yt_own.at[zz], dst_ref=yt_all.at[mine],
-                send_sem=gy_send.at[d], recv_sem=gy_recv.at[d],
-                device_id=at(x, core, zz), device_id_type=MESH),
-        )
+        return pltpu.make_async_remote_copy(
+            src_ref=yt_own.at[zz], dst_ref=yt_all.at[mine],
+            send_sem=gy_send.at[d], recv_sem=gy_recv.at[z],
+            device_id=at(x, core, zz), device_id_type=MESH)
+
+    def y_arrival(zz):
+        return pltpu.make_async_remote_copy(
+            src_ref=yt_own.at[zz], dst_ref=yt_all.at[x * Z + zz],
+            send_sem=gy_send.at[0], recv_sem=gy_recv.at[zz],
+            device_id=at(x, core, zz), device_id_type=MESH)
+
+    def pass_on(zz, act):
+        @pl.when((zz <= z) & (z < Z - 1))
+        def _():
+            act(hop(zz, 1))
+
+        @pl.when((zz >= z) & (z > 0))
+        def _():
+            act(hop(zz, 0))
 
     def upward(slot):
         return (
@@ -204,11 +220,11 @@
                 device_id=at(x + 1, core, z), device_id_type=MESH),
         )
 
-    for d in range(1, Z):
-        for copy in along(d):
-            copy.start()
     sig_all[mine] = sig_ref[...]
     yt_all[mine] = yt_own[z]
+    pass_on(z, lambda copy: copy.start())
+    for d in range(1, Z):
+        y_copy(d).start()
 
     is_first = lax.broadcasted_iota(jnp.int32, (C, 1), 0) < cols
 
@@ -221,15 +237,29 @@
             send_sem=ex_send.at[s, k], recv_sem=ex_recv.at[s, k],
             device_id=at(x, 1 - core, z), device_id_type=MESH)
 
-    def block(dz, dx):
+    def count_copy():
+        return pltpu.make_async_remote_copy(
+            src_ref=totals, dst_ref=got_totals, send_sem=t_send, recv_sem=t_recv,
+            device_id=at(x, 1 - core, z), device_id_type=MESH)
+
+    inner = jnp.minimum(z, Z - 1 - z)
+    rest = jnp.where(2 * z >= Z, -1, 1)
+
+    def nearest(i):
+        near = jnp.where(i % 2 == 1, -((i + 1) // 2), i // 2)
+        return z + jnp.where(i <= 2 * inner, near, rest * (i - inner))
+
+    def block(i, dx):
         xx = x - dx
-        zz = lax.rem(z + Z - dz, Z)
+        zz = nearest(i)
         slot = xx * Z + zz
-
-        @pl.when((dx == 0) & (dz > 0))
+        is_last = (i == Z - 1) & (dx == x)
+
+        @pl.when((dx == 0) & (i > 0))
         def _():
-            for copy in along(dz):
-                copy.wait()
+            hop(zz, 0).wait_recv()
+            pass_on(zz, lambda copy: copy.start())
+            y_arrival(zz).wait_recv()
 
         @pl.when(dx > 0)
         def _():
@@ -248,6 +278,14 @@
             allow = jnp.where(2 * xx + core <= 2 * x + q, 1.0, 0.0).astype(f32)
             msk[q, :, pl.ds(base, rows)] = jnp.broadcast_to(live * allow, (8, rows))
             lhs[q * cols:(q + 1) * cols, :] = (y * allow).astype(jnp.bfloat16)
+
+        @pl.when(is_last)
+        def _():
+            for q in range(2):
+                total = jnp.sum(msk[q], axis=1, keepdims=True)
+                totals[q] = jnp.broadcast_to(total, totals.shape[1:])
+            count_copy().start()
+
         for k in range(nch):
             part = slice(k * chunk, (k + 1) * chunk)
             proj[:, part] = mm(sig_all[slot], w_ref[:, part])
@@ -274,20 +312,11 @@
             here = pl.ds(base, rows)
             own[0, k] += mm(lhs[...], hi[here, part]) + mm(lhs[...], lo[here, part])
 
-            @pl.when((dz == Z - 1) & (dx == x))
+            @pl.when(is_last)
             def _():
                 exchange(0, k).start()
 
     own[0] = jnp.zeros((nch, C, chunk), f32)
-
-    def column(dz, carry):
-        def one(dx, carry):
-            block(dz, dx)
-            return carry
-
-        return lax.fori_loop(0, x + 1, one, carry)
-
-    lax.fori_loop(0, Z, column, 0)
 
     def absent(slot, carry):
         here = pl.ds(pl.multiple_of(slot * rows, rows), rows)
@@ -298,6 +327,23 @@
 
     lax.fori_loop((x + 1) * Z, B, absent, 0)
 
+    def column(i, carry):
+        def one(dx, carry):
+            block(i, dx)
+            return carry
+
+        return lax.fori_loop(0, x + 1, one, carry)
+
+    lax.fori_loop(0, Z, column, 0)
+
+    def passed(zz, carry):
+        pass_on(zz, lambda copy: copy.wait_send())
+        return carry
+
+    lax.fori_loop(0, Z, passed, 0)
+    for d in range(1, Z):
+        y_copy(d).wait_send()
+
     @pl.when(x < X - 1)
     def _():
         def sent(slot, carry):
@@ -307,13 +353,7 @@
 
         lax.fori_loop(0, (x + 1) * Z, sent, 0)
 
-    for q in range(2):
-        totals[q] = jnp.broadcast_to(jnp.sum(msk[q], axis=1, keepdims=True), totals.shape[1:])
-    count_copy = pltpu.make_async_remote_copy(
-        src_ref=totals, dst_ref=got_totals, send_sem=t_send, recv_sem=t_recv,
-        device_id=at(x, 1 - core, z), device_id_type=MESH)
-    count_copy.start()
-    count_copy.wait()
+    count_copy().wait()
     count = [totals[q][0:1, 0:1] + got_totals[q][0:1, 0:1] for q in range(2)]
     inverse = spread(1.0 / count[0], 1.0 / count[1])
 
@@ -477,7 +517,7 @@
         ((Z * cols, F // Z), f32), ((ITERS, Z, cols, F // Z), f32),
     ]
     held = sum(math.prod(shape) * jnp.dtype(dtype).itemsize for shape, dtype in buffers)
-    sems = [(Z,)] * 4 + [(B,)] * 4 + [(ITERS, nch)] * 2 + [()] * 2 + [(ITERS, Z)] * 2 + [(2 * Z,)] * 2 + [(ITERS, Z)] * 2
+    sems = [(2, Z)] + [(Z,)] * 3 + [(B,)] * 4 + [(ITERS, nch)] * 2 + [()] * 2 + [(ITERS, Z)] * 2 + [(2 * Z,)] * 2 + [(ITERS, Z)] * 2
     return buffers, sems, held
 
 

time: 81.2 us -> 75.7 us (0.932)
  Pallas kernels: 77.5 us -> 72.2 us
    pallas_call x1, Pallas kernels: 77.5 us -> 72.2 us  [fused(): pl.pallas_call(functools.partial(kernel, E // 2, Z, chunk, float(F * T)),...]
where the time goes in v5:
time: 75.7 us; the launch traced here: 74.7 us
  Pallas kernels  72.2 us (95%)
  local copies, waits for them, and re-layouts  1.87 us (2%)
    pallas_call x1, Pallas kernels, fused(): pl.pallas_call(functools.partial(kernel, E // 2, Z, chunk, float(F * T)),...  72.2 us
    unnamed x1, local copies, waits for them, and re-layouts  1.87 us

profile of v5, /device:TPU:11, one launch (start us, length us, event | category | flops | bytes accessed | tf_op | source)
XLA Modules:
  0.0 74.7 jit_solution(15918601483114317110)
XLA Ops:
  0.7 72.2 %shard_map.64 = f32[512,256]{1,0:T(8,128)} custom-call(s32[1,1]{1,0:T(1,128)S(6)} %copy.8.counts_ref, bf16[256,256]{1,0:T(8,128)(2,1)} %bitcast.6, bf16[256,256]{1,0:T(8,128)(2,1)} %bitcast.7, bf16[256,2048]{1,0:T(8,128)(2,1)} %w_ref.1, s32[1,2048]{1,0:T(1,128)} %bitcast.8, f32[1,2048]{1,0:T(1,128)} %bitcast.9), custom_call_target="tpu_custom_call" | custom-call | tf_op jit(solution)/shard_map/pallas_call | solution.py:547
  72.8 1.9 %copy.9 = f32[1,512,256]{2,1,0:T(8,128)} copy(f32[1,512,256]{2,1,0:T(8,128)} %bitcast.5) | data formatting | bytes 1048576

commit v6 on v5

--- a/solution.py
+++ b/solution.py
@@ -308,12 +308,13 @@
                 lo[to, part] = low
                 return carry
 
-            lax.fori_loop(0, rows // 16, strip, 0, unroll=4)
+            lax.fori_loop(0, rows // 16, strip, 0, unroll=rows // 16)
             here = pl.ds(base, rows)
             own[0, k] += mm(lhs[...], hi[here, part]) + mm(lhs[...], lo[here, part])
 
-            @pl.when(is_last)
-            def _():
+        @pl.when(is_last)
+        def _():
+            for k in range(nch):
                 exchange(0, k).start()
 
     own[0] = jnp.zeros((nch, C, chunk), f32)
@@ -416,11 +417,15 @@
             part = slice(k * chunk, (k + 1) * chunk)
             high, low = split(u_now[:, part])
             ust[0:C, part] = high
-            ust[C:2 * C, part] = low
+            if it == 0:
+                ust[C:2 * C, part] = low
         for k in range(nch):
             part = slice(k * chunk, (k + 1) * chunk)
-            image = mm(ust[...], hi[:, part])
-            own[s, k] = image[0:C] + image[C:] + mm(ust[0:C, :], lo[:, part])
+            if it == 0:
+                image = mm(ust[...], hi[:, part])
+                own[s, k] = image[0:C] + image[C:] + mm(ust[0:C, :], lo[:, part])
+            else:
+                own[s, k] = mm(ust[0:C, :], hi[:, part])
             exchange(s, k).start()
         curve = jnp.zeros((C, 1), f32)
         for k in range(nch):

time: 75.7 us -> 73.6 us (0.972)
  Pallas kernels: 72.2 us -> 70.1 us
    pallas_call x1, Pallas kernels: 72.2 us -> 70.1 us  [fused(): pl.pallas_call(functools.partial(kernel, E // 2, Z, chunk, float(F * T)),...]
where the time goes in v6:
time: 73.6 us; the launch traced here: 72.6 us
  Pallas kernels  70.1 us (95%)
  local copies, waits for them, and re-layouts  1.87 us (3%)
    pallas_call x1, Pallas kernels, fused(): pl.pallas_call(functools.partial(kernel, E // 2, Z, chunk, float(F * T)),...  70.1 us
    unnamed x1, local copies, waits for them, and re-layouts  1.87 us

profile of v6, /device:TPU:11, one launch (start us, length us, event | category | flops | bytes accessed | tf_op | source)
XLA Modules:
  0.0 72.6 jit_solution(7027452910198605033)
XLA Ops:
  0.7 70.1 %shard_map.64 = f32[512,256]{1,0:T(8,128)} custom-call(s32[1,1]{1,0:T(1,128)S(6)} %copy.8.counts_ref, bf16[256,256]{1,0:T(8,128)(2,1)} %bitcast.6, bf16[256,256]{1,0:T(8,128)(2,1)} %bitcast.7, bf16[256,2048]{1,0:T(8,128)(2,1)} %w_ref.1, s32[1,2048]{1,0:T(1,128)} %bitcast.8, f32[1,2048]{1,0:T(1,128)} %bitcast.9), custom_call_target="tpu_custom_call" | custom-call | tf_op jit(solution)/shard_map/pallas_call | solution.py:552
  70.7 1.9 %copy.9 = f32[1,512,256]{2,1,0:T(8,128)} copy(f32[1,512,256]{2,1,0:T(8,128)} %bitcast.5) | data formatting | bytes 1048576
